TPU v7x, 512 devices: a whole 4x4x16 slice. The times are simulated.
512 devices in a mesh: heads: 8 (over x, z_hi), tokens: 64 (over y, z_lo, core).
Axes of the slice: x: 4, y: 4, z: 16 (z_hi: 2, z_lo: 8; z = z_hi * 8 + z_lo), core: 2. Of those that a mesh axis runs over, the one named last changes fastest.
Arguments:
- queries: bfloat16 [128, 64, 576], P('heads', 'tokens'), may hold values from -40 to 40
- latent_keys: bfloat16 [65536, 576], P('tokens'), may hold values from -4 to 4
- index_queries: bfloat16 [64, 64, 128], P(None, 'heads'), may hold values from -4 to 4
- index_keys: bfloat16 [65536, 128], P('tokens'), may hold values from -8 to 8
- index_weights: float32 [64, 64], P(None, 'heads'), may hold values from 0 to 1.2
- positions: int32 [64], replicated, may hold values from 32768 to 65535
Outputs:
- index_query_grad: float32 [64, 64, 128], P(None, 'heads')
- index_weight_grad: float32 [64, 64], P(None, 'heads')
- index_key_grad: float32 [65536, 128], P('tokens')
All inputs are finite; a program needn't handle non-finite values.
Results may differ from a plain program's by a relative error of at most 0.0026.
Values may be sent and summed in bfloat16 or wider, within the bound.
No kernel may reach another device: no remote copies, remote signals or barrier semaphores. Data moves between devices by JAX's collectives and lax.ppermute only.
A program may use at most 64 MiB of HBM per device.

v0:
```python
import jax
import jax.numpy as jnp
from jax import lax
from jax.sharding import PartitionSpec as P

H = 128
softmax_scale = 192.0 ** (-0.5)
masked_value = -1e30


def sent_to_all(value, axis):
    devices = lax.axis_size(axis)
    return lax.all_to_all(
        jnp.broadcast_to(value[None], (devices, *value.shape)), axis, 0, 0, tiled=True
    )


def gathered_once(value, axis):
    leaves = jax.tree.leaves(value)
    order = sorted(range(len(leaves)), key=lambda k: -leaves[k].size)
    width = (1, *leaves[order[0]].shape)[-1]
    lines = [
        jnp.pad(leaves[k].reshape(-1), (0, -leaves[k].size % width)).reshape(-1, width)
        for k in order
    ]
    both, at, found = (sent_to_all(jnp.concatenate(lines), axis), 0, {})
    for k, line in zip(order, lines):
        slab = both[:, at : at + len(line)].reshape(len(both), -1)
        found[k] = slab[:, : leaves[k].size].reshape(-1, *leaves[k].shape)
        at += len(line)
    numbers = iter(range(len(leaves)))
    return jax.tree.map(lambda _: found[next(numbers)], value)


def folded_in_pairs(pieces, combine):
    while len(jax.tree.leaves(pieces)[0]) > 1:
        pieces = jax.vmap(combine)(
            *(jax.tree.map(lambda part: part[side::2], pieces) for side in (0, 1))
        )
    return jax.tree.map(lambda part: part[0], pieces)


def combined_all(value, axis, combine):
    pieces = gathered_once(value, axis)
    return folded_in_pairs(pieces, combine)


def cut_along(value, dim, devices):
    before, after = (value.shape[:dim], value.shape[dim + 1 :])
    return jnp.moveaxis(value.reshape(*before, devices, -1, *after), dim, 0)


def one_scatter(arrays, axis, dims):
    devices = lax.axis_size(axis)
    parts = [cut_along(a, dim, devices) for a, dim in zip(arrays, dims)]
    lines = jnp.concatenate([b.reshape(devices, -1) for b in parts], axis=1)
    rows = max(16, -(-lines.shape[1] // 1024) * 8)
    lines = jnp.pad(lines, ((0, 0), (0, rows * 128 - lines.shape[1]))).reshape(-1, 128)
    vector, at, outs = (lax.psum_scatter(lines, axis, tiled=True).reshape(-1), 0, [])
    for b in parts:
        part = b[0]
        outs.append(vector[at : at + part.size].reshape(part.shape))
        at += part.size
    return tuple(outs)


def in_order(parts, dim):
    dims = list(parts.shape[1:])
    dims[dim] *= parts.shape[0]
    return jnp.moveaxis(parts, 0, dim).reshape(dims)


def gathered_copies(value, axis, dim):
    parts = sent_to_all(value, axis)
    return in_order(parts, dim)


def padded_to(lines, devices):
    spare = -len(lines) % devices
    return jnp.pad(lines, [(0, spare)] + [(0, 0)] * (lines.ndim - 1))


def sent_and_summed(value, axis, dim):
    parts = cut_along(value, dim, lax.axis_size(axis))
    arrived = lax.all_to_all(parts, axis, split_axis=0, concat_axis=0, tiled=True)
    return arrived.sum(axis=0)


def nested_sum(value, axes):
    lines = value.reshape(-1, value.shape[-1])
    padded = padded_to(lines, lax.axis_size(axes))
    whole = gathered_copies(sent_and_summed(padded, axes, 0), axes, 0)
    return lax.slice_in_dim(whole, 0, len(lines)).reshape(value.shape)


def block_size(heads_here, row_limit):
    chosen = 1
    for option in range(1, heads_here + 1):
        if heads_here % option == 0 and option <= row_limit:
            chosen = option
    return chosen


def joined_stats(first_pair, second_pair):
    maximum = jnp.maximum(first_pair[0], second_pair[0])
    totals = first_pair[1] * jnp.exp(first_pair[0] - maximum) + second_pair[1] * jnp.exp(
        second_pair[0] - maximum
    )
    return (maximum, totals)


def global_stats(local_max, local_total):
    maximum, totals = combined_all((local_max, local_total), "tokens", joined_stats)
    return (maximum, totals)


def logit_grad(summed_target, logits, visible, loss_scale):
    target = summed_target / H
    masked = jnp.where(visible, logits, masked_value)
    local_max = jnp.max(masked, axis=1)
    local_total = jnp.sum(jnp.exp(masked - local_max[:, None]), axis=1)
    maximum, totals = global_stats(local_max, local_total)
    index_probs = jnp.exp(masked - maximum[:, None]) / totals[:, None]
    return loss_scale * (index_probs - target)


def local(queries, latent_keys, index_queries, index_keys, index_weights, positions):
    key_count = latent_keys.shape[0]
    loss_scale = key_count * lax.axis_size("tokens") // 8
    offset = lax.axis_index("tokens") * key_count
    key_index = offset + jnp.arange(key_count, dtype=jnp.int32)
    visible = key_index[None, :] <= positions[:, None]
    gathered = lax.all_gather(queries, "tokens", axis=1, tiled=True)
    head_count, query_count, width_qk = gathered.shape
    per_block = block_size(head_count, max(1, 512 // query_count))
    head_blocks = gathered.reshape(head_count // per_block, per_block, query_count, width_qk)

    def block_scores(head_block):
        scores = (
            jnp.einsum("hqd,kd->hqk", head_block, latent_keys, preferred_element_type=jnp.float32)
            * softmax_scale
        )
        return jnp.where(visible[None], scores, masked_value)

    def block_stats(head_block):
        scores = block_scores(head_block)
        maximum = jnp.max(scores, axis=2)
        return (maximum, jnp.sum(jnp.exp(scores - maximum[..., None]), axis=2))

    local_max, local_total = lax.map(block_stats, head_blocks)
    head_max, head_total = global_stats(local_max, local_total)

    def accumulate(running, inputs):
        head_block, maximum, totals = inputs
        scores = block_scores(head_block)
        probabilities = jnp.exp(scores - maximum[..., None]) / totals[..., None]
        return (running + jnp.sum(probabilities, axis=0), None)

    partial_target, _ = lax.scan(
        accumulate,
        jnp.zeros((query_count, key_count), jnp.float32),
        (head_blocks, head_max, head_total),
    )
    index_scale = index_queries.shape[2] ** (-0.5)
    active = (
        jnp.einsum("qjd,kd->qjk", index_queries, index_keys, preferred_element_type=jnp.float32)
        * index_scale
    )
    rectified = jnp.maximum(active, 0.0)
    partial_logits = jnp.sum(index_weights[:, :, None] * rectified, axis=1)
    row_count = query_count // lax.axis_size("heads")
    share_target, share_logits = one_scatter((partial_target, partial_logits), "heads", (0, 0))
    first_row = lax.axis_index("heads") * row_count
    share_visible = lax.dynamic_slice_in_dim(visible, first_row, row_count, 0)
    share_grad = logit_grad(share_target, share_logits, share_visible, loss_scale)
    dlogit = gathered_copies(share_grad, "heads", 0)
    gate_grad = (dlogit[:, None, :] * index_weights[:, :, None] * (active > 0.0)).astype(
        jnp.bfloat16
    )
    query_local = (
        jnp.einsum("qjk,kd->qjd", gate_grad, index_keys, preferred_element_type=jnp.float32)
        * index_scale
    )
    weight_local = jnp.sum(dlogit[:, None, :] * rectified, axis=2)
    query_grad, weight_grad = (
        nested_sum(query_local, "tokens"),
        nested_sum(weight_local, "tokens"),
    )
    key_local = (
        jnp.einsum("qjk,qjd->kd", gate_grad, index_queries, preferred_element_type=jnp.float32)
        * index_scale
    )
    key_grad = lax.psum(key_local, "heads")
    return (query_grad, weight_grad, key_grad)


def solution(mesh):
    placed = (
        P("heads", "tokens", None),
        P("tokens", None),
        P(None, "heads", None),
        P("tokens", None),
        P(None, "heads"),
        P(),
    )
    return jax.shard_map(
        local,
        mesh=mesh,
        in_specs=placed,
        out_specs=(P(None, "heads", None), P(None, "heads"), P("tokens", None)),
        check_vma=False,
    )
```

profile of v0, /device:TPU:1, one launch (start us, length us, event | category | flops | bytes accessed | tf_op | source)
XLA Modules:
  0.0 615.3 jit_solution(9117610947227083281)
XLA Ops:
  7.2 0.7 all-gather.2.cloned.1.call-update
  8.0 128.1 %all-gather.2.cloned.1.call-done = bf16[16,64,576]{2,0,1:T(8,128)(2,1)} async-done(((bf16[16,1,576]{2,0,1:T(8,128)(2,1)}), bf16[16,64,576]{2,0,1:T(8,128)(2,1)}) %all-gather.2.cloned.1.call-update) | async-done | bytes 1179664 | tf_op jit(solution)/shard_map/all_gather | solution.py:133
  136.0 1.6 copy.14
  137.7 3.7 while.24
  137.7 0.1 broadcast_compare_fusion.4
  137.8 1.1 fusion.30
  138.9 0.6 exponential_reduce_fusion.3
  139.5 0.1 broadcast_compare_fusion.4
  139.7 1.1 fusion.30
  140.8 0.6 exponential_reduce_fusion.3
  141.4 1.0 copy-done.2
  142.5 0.1 broadcast_in_dim.75
  142.6 1.5 reshape.94
  144.1 7.3 %all-to-all-start = ((f32[64,1,2048]{2,1,0:T(1,128)}), f32[64,1,2048]{2,1,0:T(1,128)S(1)}, u32[]{:S(2)}, u32[]{:S(2)}) async-start(f32[64,1,2048]{2,1,0:T(1,128)} %reshape.94), calls=%async_computation | async-start | bytes 1048576 | tf_op jit(solution)/shard_map/all_to_all | solution.py:13
  151.5 0.1 copy.15
  151.6 1.6 multiply_reduce_fusion.1
  153.2 1.0 reshape_reshape.15
  154.2 26.9 %all-to-all-done = f32[64,1,2048]{2,1,0:T(1,128)S(1)} async-done(((f32[64,1,2048]{2,1,0:T(1,128)}), f32[64,1,2048]{2,1,0:T(1,128)S(1)}, u32[]{:S(2)}, u32[]{:S(2)}) %all-to-all-start) | async-done | bytes 524320 | tf_op jit(solution)/shard_map/all_to_all | solution.py:13
  181.0 0.8 copy-done.1
  181.8 0.5 broadcast.50
  182.3 2.9 reduce.1
  185.3 1.4 reshape.95
  186.7 1.3 slice_bitcast_fusion.1
  187.9 0.1 multiply_add_fusion
  188.0 0.1 multiply_add_fusion.1
  188.2 6.0 while.25
  188.2 0.1 broadcast_compare_fusion.5
  188.4 2.8 fusion.33
  191.1 0.1 select_add_fusion.2
  191.3 0.1 broadcast_compare_fusion.5
  191.4 2.8 fusion.33
  194.2 0.1 select_add_fusion.2
  194.3 0.1 reshape_reshape.14
  194.4 0.9 reshape.82
  195.3 0.1 dynamic-slice
  195.4 106.3 %reduce-scatter.2.cloned.1.call-done = f32[128,128]{1,0:T(8,128)} async-done(((f32[1024,128]{1,0:T(8,128)}), f32[128,128]{1,0:T(8,128)}) %reduce-scatter.2.cloned.1.call-update) | async-done | bytes 65552 | tf_op jit(solution)/shard_map/reduce_scatter | solution.py:59
  301.6 0.8 fusion.23
  302.4 0.2 fusion.19
  302.6 0.2 exponential_reduce_fusion.1
  302.8 0.7 broadcast_in_dim.77
  303.5 7.3 %all-to-all-start.1 = ((f32[64,2,8]{2,1,0:T(2,128)}), f32[64,2,8]{2,1,0:T(2,128)S(1)}, u32[]{:S(2)}, u32[]{:S(2)}) async-start(f32[64,2,8]{2,1,0:T(2,128)} %broadcast_in_dim.77), calls=%async_computation.2 | async-start | bytes 131072 | tf_op jit(solution)/shard_map/all_to_all | solution.py:13
  310.8 12.8 %all-to-all-done.1 = f32[64,2,8]{2,1,0:T(2,128)S(1)} async-done(((f32[64,2,8]{2,1,0:T(2,128)}), f32[64,2,8]{2,1,0:T(2,128)S(1)}, u32[]{:S(2)}, u32[]{:S(2)}) %all-to-all-start.1) | async-done | bytes 4128 | tf_op jit(solution)/shard_map/all_to_all | solution.py:13
  323.6 0.1 fusion.22
  324.2 0.1 subtract_multiply_fusion
  324.3 24.4 %all_to_all.35 = f32[8,8,1024]{2,1,0:T(8,128)S(1)} all-to-all(f32[8,8,1024]{2,1,0:T(8,128)S(1)} %broadcast_in_dim.78), channel_id=1, replica_groups=mesh['heads'=8,'tokens'=64] {'heads'}, dimensions={0} | all-to-all | bytes 524288 | tf_op jit(solution)/shard_map/all_to_all | solution.py:13
  348.7 1.0 multiply_reduce_fusion
  349.7 13.4 %all-to-all-start.5 = ((f32[64,1,8]{2,1,0:T(1,128)}), f32[64,1,8]{2,1,0:T(1,128)S(1)}, u32[]{:S(2)}, u32[]{:S(2)}) async-start(f32[64,1,8]{2,1,0:T(1,128)} %bitcast.15), calls=%async_computation.6 | async-start | bytes 65536 | tf_op jit(solution)/shard_map/all_to_all | solution.py:85
  363.2 1.2 convolution_multiply_fusion
  364.4 11.0 %all-to-all-done.5 = f32[64,1,8]{2,1,0:T(1,128)S(1)} async-done(((f32[64,1,8]{2,1,0:T(1,128)}), f32[64,1,8]{2,1,0:T(1,128)S(1)}, u32[]{:S(2)}, u32[]{:S(2)}) %all-to-all-start.5) | async-done | bytes 2080 | tf_op jit(solution)/shard_map/all_to_all | solution.py:85
  375.3 4.9 all-to-all-start.3
  380.2 0.1 reduce_sum.67
  380.3 19.3 %all-to-all-done.3 = f32[64,8,128]{2,1,0:T(8,128)S(1)} async-done(((f32[64,8,128]{2,1,0:T(8,128)}), f32[64,8,128]{2,1,0:T(8,128)S(1)}, u32[]{:S(2)}, u32[]{:S(2)}) %all-to-all-start.3) | async-done | bytes 262176 | tf_op jit(solution)/shard_map/all_to_all | solution.py:85
  399.6 0.6 broadcast_in_dim.80
  400.2 6.9 %all-to-all-start.6 = ((f32[64,1,8]{2,1,0:T(1,128)}), f32[64,1,8]{2,1,0:T(1,128)S(1)}, u32[]{:S(2)}, u32[]{:S(2)}) async-start(f32[64,1,8]{2,1,0:T(1,128)} %broadcast_in_dim.80), calls=%async_computation.7 | async-start | bytes 65536 | tf_op jit(solution)/shard_map/all_to_all | solution.py:13
  407.1 0.1 reduce_sum.65
  407.2 12.1 %all-to-all-done.6 = f32[64,1,8]{2,1,0:T(1,128)S(1)} async-done(((f32[64,1,8]{2,1,0:T(1,128)}), f32[64,1,8]{2,1,0:T(1,128)S(1)}, u32[]{:S(2)}, u32[]{:S(2)}) %all-to-all-start.6) | async-done | bytes 2080 | tf_op jit(solution)/shard_map/all_to_all | solution.py:13
  419.3 0.7 broadcast_in_dim.79
  420.0 4.7 all-to-all-start.4
  424.8 1.5 fusion.15
  426.4 0.7 copy.19
  427.0 17.1 %all-to-all-done.4 = f32[64,8,128]{2,1,0:T(8,128)S(1)} async-done(((f32[64,8,128]{2,1,0:T(8,128)}), f32[64,8,128]{2,1,0:T(8,128)S(1)}, u32[]{:S(2)}, u32[]{:S(2)}) %all-to-all-start.4) | async-done | bytes 262176 | tf_op jit(solution)/shard_map/all_to_all | solution.py:13
  444.1 162.1 %all-reduce.2.cloned.1.call-done = f32[1024,128]{1,0:T(8,128)} async-done(((f32[1024,128]{1,0:T(8,128)}), f32[1024,128]{1,0:T(8,128)}) %all-reduce.2.cloned.1.call-update) | async-done | bytes 524304 | tf_op jit(solution)/shard_map/psum | solution.py:193
  606.2 0.7 copy.42
  606.9 1.9 copy.43
  (63 shorter events, 0.9 us)
Async XLA Ops:
  7.2 144.4 %copy-start = (bf16[1024,128]{1,0:T(8,128)(2,1)S(1)}, bf16[1024,128]{1,0:T(8,128)(2,1)}, u32[]{:S(2)}) copy-start(bf16[1024,128]{1,0:T(8,128)(2,1)} %param.13) | copy-start | bytes 786436
  7.2 130.5 %copy-start.7 = (bf16[1024,576]{0,1:T(8,128)(2,1)S(1)}, bf16[1024,576]{0,1:T(8,128)(2,1)}, u32[]{:S(2)}) copy-start(bf16[1024,576]{0,1:T(8,128)(2,1)} %param.11) | copy-start | bytes 3538948
  7.2 130.5 %copy-start.5 = (s32[64]{0:T(128)S(1)}, s32[64]{0:T(128)}, u32[]{:S(2)}) copy-start(s32[64]{0:T(128)} %param.15) | copy-start | bytes 772
  7.2 128.8 %all-gather.2.cloned.1.call-start = ((), (), s32[]{:S(2)}) async-start(), calls=%async_computation.8 | async-start | bytes 1331200 | tf_op jit(solution)/shard_map/all_gather | solution.py:133
  141.4 1.1 copy-start.2
  141.4 10.1 %copy-start.6 = (f32[64,8]{0,1:T(8,128)S(1)}, f32[64,8]{0,1:T(8,128)}, u32[]{:S(2)}) copy-start(f32[64,8]{0,1:T(8,128)} %param.14) | copy-start | bytes 6148
  141.4 10.1 %copy-start.3 = (bf16[64,8,128]{2,1,0:T(8,128)(2,1)S(1)}, bf16[64,8,128]{2,1,0:T(8,128)(2,1)}, u32[]{:S(2)}) copy-start(bf16[64,8,128]{2,1,0:T(8,128)(2,1)} %param.12) | copy-start | bytes 393220
  144.1 37.0 %all-to-all-start = ((f32[64,1,2048]{2,1,0:T(1,128)}), f32[64,1,2048]{2,1,0:T(1,128)S(1)}, u32[]{:S(2)}, u32[]{:S(2)}) async-start(f32[64,1,2048]{2,1,0:T(1,128)} %reshape.94), calls=%async_computation | async-start | bytes 1048576 | tf_op jit(solution)/shard_map/all_to_all | solution.py:13
  151.4 150.2 %reduce-scatter.2.cloned.1.call-start = ((), (), s32[]{:S(2)}) async-start(), calls=%async_computation.9 | async-start | bytes 589824 | tf_op jit(solution)/shard_map/reduce_scatter | solution.py:59
  181.0 0.8 copy-start.1
  303.5 20.2 %all-to-all-start.1 = ((f32[64,2,8]{2,1,0:T(2,128)}), f32[64,2,8]{2,1,0:T(2,128)S(1)}, u32[]{:S(2)}, u32[]{:S(2)}) async-start(f32[64,2,8]{2,1,0:T(2,128)} %broadcast_in_dim.77), calls=%async_computation.2 | async-start | bytes 131072 | tf_op jit(solution)/shard_map/all_to_all | solution.py:13
  349.7 25.6 %all-to-all-start.5 = ((f32[64,1,8]{2,1,0:T(1,128)}), f32[64,1,8]{2,1,0:T(1,128)S(1)}, u32[]{:S(2)}, u32[]{:S(2)}) async-start(f32[64,1,8]{2,1,0:T(1,128)} %bitcast.15), calls=%async_computation.6 | async-start | bytes 65536 | tf_op jit(solution)/shard_map/all_to_all | solution.py:85
  363.1 61.6 %copy-start.4 = (bf16[64,8,128]{2,1,0:T(8,128)(2,1)S(1)}, bf16[64,8,128]{2,1,0:T(8,128)(2,1)}, u32[]{:S(2)}) copy-start(bf16[64,8,128]{2,1,0:T(8,128)(2,1)} %param.12) | copy-start | bytes 393220
  375.3 24.3 %all-to-all-start.3 = ((f32[64,8,128]{2,1,0:T(8,128)}), f32[64,8,128]{2,1,0:T(8,128)S(1)}, u32[]{:S(2)}, u32[]{:S(2)}) async-start(f32[64,8,128]{2,1,0:T(8,128)} %convolution_multiply_fusion), calls=%async_computation.4 | async-start | bytes 524288 | tf_op jit(solution)/shard_map/all_to_all | solution.py:85
  400.2 19.1 %all-to-all-start.6 = ((f32[64,1,8]{2,1,0:T(1,128)}), f32[64,1,8]{2,1,0:T(1,128)S(1)}, u32[]{:S(2)}, u32[]{:S(2)}) async-start(f32[64,1,8]{2,1,0:T(1,128)} %broadcast_in_dim.80), calls=%async_computation.7 | async-start | bytes 65536 | tf_op jit(solution)/shard_map/all_to_all | solution.py:13
  420.0 24.1 %all-to-all-start.4 = ((f32[64,8,128]{2,1,0:T(8,128)}), f32[64,8,128]{2,1,0:T(8,128)S(1)}, u32[]{:S(2)}, u32[]{:S(2)}) async-start(f32[64,8,128]{2,1,0:T(8,128)} %broadcast_in_dim.79), calls=%async_computation.5 | async-start | bytes 524288 | tf_op jit(solution)/shard_map/all_to_all | solution.py:13
  424.7 181.5 %all-reduce.2.cloned.1.call-start = ((), (), s32[]{:S(2)}) async-start(), calls=%async_computation.10 | async-start | bytes 1048576 | tf_op jit(solution)/shard_map/psum | solution.py:193
Sparse Core Ops, SparseCore 0:
  10.2 125.8 all-gather.1
  195.4 106.1 reduce-scatter.1
  429.3 176.8 all-reduce.1
where the time goes:
time: 616 us; the launch traced here: 615 us
  waiting for transfers between devices  496 us (81%)
  starting transfers between devices  44.7 us (7%)
  blocking collectives  24.4 us (4%)
  local copies, waits for them, and re-layouts  16 us (3%)
  between operations  14.1 us (2%)
  matrix products  12.1 us (2%)
  other arithmetic  7.47 us (1%)
    psum x1, waiting for transfers between devices, local(): key_grad = lax.psum(key_local, 'heads')  162 us
    all_gather x1, waiting for transfers between devices, local(): gathered = lax.all_gather(queries, 'tokens', axis=1, tiled=True)  128 us
    reduce_scatter x1, waiting for transfers between devices, one_scatter(): lax.psum_scatter(lines, axis, tiled=True).reshape(-1)  106 us
    all_to_all x4, waiting for transfers between devices, sent_to_all(): lax.all_to_all(jnp.broadcast_to(value[None], (devices, *value.shape)), ax...  68.9 us
    all_to_all x2, waiting for transfers between devices, sent_and_summed(): lax.all_to_all(parts, axis, split_axis=0, concat_axis=0, tiled=True)  30.3 us
    all_to_all x4, starting transfers between devices, sent_to_all(): lax.all_to_all(jnp.broadcast_to(value[None], (devices, *value.shape)), ax...  26.3 us
    all_to_all x1, blocking collectives, sent_to_all(): lax.all_to_all(jnp.broadcast_to(value[None], (devices, *value.shape)), ax...  24.4 us
    all_to_all x2, starting transfers between devices, sent_and_summed(): lax.all_to_all(parts, axis, split_axis=0, concat_axis=0, tiled=True)  18.3 us
  transfers between devices with their start and end apart: 9, of which 9 were waited for; matrix products, arithmetic and copies ran while one was open for 1% of the time, Pallas kernels for 0%

commit v1 on v0

--- a/solution.py
+++ b/solution.py
@@ -190,7 +190,7 @@
         jnp.einsum("qjk,qjd->kd", gate_grad, index_queries, preferred_element_type=jnp.float32)
         * index_scale
     )
-    key_grad = lax.psum(key_local, "heads")
+    key_grad = jnp.sum(lax.all_gather(key_local, "heads"), axis=0)
     return (query_grad, weight_grad, key_grad)
 
 

time: 616 us -> 562 us (0.912)
  waiting for transfers between devices: 496 us -> 421 us
  starting transfers between devices: 44.7 us -> 62.3 us
    psum x1 -> x0, waiting for transfers between devices: 162 us -> none  [local(): key_grad = lax.psum(key_local, 'heads')]
    all_to_all x4, waiting for transfers between devices: 68.9 us -> 154 us  [sent_to_all(): lax.all_to_all(jnp.broadcast_to(value[None], (devices, *value.shape)), ax...]
    all_to_all x2, starting transfers between devices: 18.3 us -> 37.2 us  [sent_and_summed(): lax.all_to_all(parts, axis, split_axis=0, concat_axis=0, tiled=True)]
  transfers between devices with their start and end apart: 9 -> 9, of which waited for: 9 -> 8; matrix products, arithmetic and copies ran while one was open for 1% -> 1% of each run, Pallas kernels for 0% -> 0%
where the time goes in v1:
time: 562 us; the launch traced here: 561 us
  waiting for transfers between devices  421 us (75%)
  starting transfers between devices  62.3 us (11%)
  blocking collectives  24.5 us (4%)
  matrix products  14.7 us (3%)
  local copies, waits for them, and re-layouts  14.2 us (3%)
  between operations  14.1 us (3%)
  other arithmetic  10.7 us (2%)
    all_to_all x4, waiting for transfers between devices, sent_to_all(): lax.all_to_all(jnp.broadcast_to(value[None], (devices, *value.shape)), ax...  154 us
    all_gather x1, waiting for transfers between devices, local(): gathered = lax.all_gather(queries, 'tokens', axis=1, tiled=True)  128 us
    reduce_scatter x1, waiting for transfers between devices, one_scatter(): lax.psum_scatter(lines, axis, tiled=True).reshape(-1)  106 us
    all_to_all x2, starting transfers between devices, sent_and_summed(): lax.all_to_all(parts, axis, split_axis=0, concat_axis=0, tiled=True)  37.2 us
    all_to_all x2, waiting for transfers between devices, sent_and_summed(): lax.all_to_all(parts, axis, split_axis=0, concat_axis=0, tiled=True)  31 us
    all_to_all x4, starting transfers between devices, sent_to_all(): lax.all_to_all(jnp.broadcast_to(value[None], (devices, *value.shape)), ax...  25 us
    all_to_all x1, blocking collectives, sent_to_all(): lax.all_to_all(jnp.broadcast_to(value[None], (devices, *value.shape)), ax...  24.5 us
  transfers between devices with their start and end apart: 9, of which 8 were waited for; matrix products, arithmetic and copies ran while one was open for 1% of the time, Pallas kernels for 0%

profile of v1, /device:TPU:1, one launch (start us, length us, event | category | flops | bytes accessed | tf_op | source)
XLA Modules:
  0.0 561.1 jit_solution(13351397635609471485)
XLA Ops:
  7.2 0.7 all-gather.4.cloned.1.call-update
  8.0 128.1 %all-gather.4.cloned.1.call-done = bf16[16,64,576]{2,0,1:T(8,128)(2,1)} async-done(((bf16[16,1,576]{2,0,1:T(8,128)(2,1)}), bf16[16,64,576]{2,0,1:T(8,128)(2,1)}) %all-gather.4.cloned.1.call-update) | async-done | bytes 1179664 | tf_op jit(solution)/shard_map/all_gather | solution.py:133
  136.0 1.6 copy.14
  137.6 6.3 %while.24 = (s32[]{:T(128)}, f32[2,8,64]{2,1,0:T(8,128)S(1)}, f32[2,8,64]{2,1,0:T(8,128)S(1)}, bf16[2,8,64,576]{3,2,1,0:T(8,128)(2,1)S(1)}, bf16[1024,576]{0,1:T...) while((s32[]{:T(128)}, f32[2,8,64]{2,1,0:T(8,128)S(1)}, ...), condition=%wide.region_3.4_spmd.clone, body=%wide.region_0.3_spmd.clone.sunk | while | flops 607714304 | bytes 6252901 | solution.py:150
  137.7 0.1 broadcast_compare_fusion.4
  137.8 2.4 fusion.30
  140.2 0.6 exponential_reduce_fusion.3
  140.8 0.1 broadcast_compare_fusion.4
  140.9 2.4 fusion.30
  143.3 0.6 exponential_reduce_fusion.3
  144.0 1.0 copy-done.2
  145.0 0.1 broadcast_in_dim.75
  145.1 1.5 reshape.95
  146.6 7.3 %all-to-all-start = ((f32[64,1,2048]{2,1,0:T(1,128)}), f32[64,1,2048]{2,1,0:T(1,128)S(1)}, u32[]{:S(2)}, u32[]{:S(2)}) async-start(f32[64,1,2048]{2,1,0:T(1,128)} %reshape.95), calls=%async_computation | async-start | bytes 1048576 | tf_op jit(solution)/shard_map/all_to_all | solution.py:13
  154.0 0.1 copy.15
  154.1 1.6 multiply_reduce_fusion.1
  155.7 1.0 reshape_reshape.15
  156.7 26.9 %all-to-all-done = f32[64,1,2048]{2,1,0:T(1,128)S(1)} async-done(((f32[64,1,2048]{2,1,0:T(1,128)}), f32[64,1,2048]{2,1,0:T(1,128)S(1)}, u32[]{:S(2)}, u32[]{:S(2)}) %all-to-all-start) | async-done | bytes 524320 | tf_op jit(solution)/shard_map/all_to_all | solution.py:13
  183.6 0.8 copy-done.1
  184.3 0.5 broadcast.50
  184.9 2.9 reduce.1
  187.8 1.4 reshape.96
  189.2 1.3 slice_bitcast_fusion.1
  190.5 0.1 multiply_add_fusion
  190.6 0.1 multiply_add_fusion.1
  190.7 6.0 %while.25 = (s32[]{:T(128)}, f32[64,1024]{1,0:T(8,128)S(1)}, bf16[2,8,64,576]{3,2,1,0:T(8,128)(2,1)}, bf16[1024,576]{0,1:T(8,128)(2,1)}, f32[2,8,64]{2,1,0:T(8,1...) while((s32[]{:T(128)}, f32[64,1024]{1,0:T(8,128)S(1)}, ...), condition=%wide.region_6.7_spmd.clone, body=%wide.region_4.6_spmd.clone.sunk | while | flops 606732288 | bytes 3031423 | solution.py:159
  190.8 0.1 broadcast_compare_fusion.5
  190.9 2.8 fusion.33
  193.6 0.1 select_add_fusion.2
  193.8 0.1 broadcast_compare_fusion.5
  193.9 2.8 fusion.33
  196.7 0.1 select_add_fusion.2
  196.8 0.1 reshape_reshape.14
  196.9 0.9 reshape.82
  197.8 0.1 dynamic-slice
  197.9 106.3 %reduce-scatter.2.cloned.1.call-done = f32[128,128]{1,0:T(8,128)} async-done(((f32[1024,128]{1,0:T(8,128)}), f32[128,128]{1,0:T(8,128)}) %reduce-scatter.2.cloned.1.call-update) | async-done | bytes 65552 | tf_op jit(solution)/shard_map/reduce_scatter | solution.py:59
  304.2 0.8 fusion.23
  305.0 0.2 fusion.19
  305.2 0.2 exponential_reduce_fusion.1
  305.4 0.7 broadcast_in_dim.77
  306.0 7.3 %all-to-all-start.1 = ((f32[64,2,8]{2,1,0:T(2,128)}), f32[64,2,8]{2,1,0:T(2,128)S(1)}, u32[]{:S(2)}, u32[]{:S(2)}) async-start(f32[64,2,8]{2,1,0:T(2,128)} %broadcast_in_dim.77), calls=%async_computation.2 | async-start | bytes 131072 | tf_op jit(solution)/shard_map/all_to_all | solution.py:13
  313.4 0.0 all-gather.6.cloned.1.call-start
  313.4 12.8 %all-to-all-done.1 = f32[64,2,8]{2,1,0:T(2,128)S(1)} async-done(((f32[64,2,8]{2,1,0:T(2,128)}), f32[64,2,8]{2,1,0:T(2,128)S(1)}, u32[]{:S(2)}, u32[]{:S(2)}) %all-to-all-start.1) | async-done | bytes 4128 | tf_op jit(solution)/shard_map/all_to_all | solution.py:13
  326.2 0.1 fusion.22
  326.7 0.1 subtract_multiply_fusion
  326.9 24.5 %all_to_all.35 = f32[8,8,1024]{2,1,0:T(8,128)S(1)} all-to-all(f32[8,8,1024]{2,1,0:T(8,128)S(1)} %broadcast_in_dim.78), channel_id=1, replica_groups=mesh['heads'=8,'tokens'=64] {'heads'}, dimensions={0} | all-to-all | bytes 524288 | tf_op jit(solution)/shard_map/all_to_all | solution.py:13
  351.4 1.5 fusion.15
  352.9 1.0 multiply_reduce_fusion
  353.9 13.4 %all-to-all-start.5 = ((f32[64,1,8]{2,1,0:T(1,128)}), f32[64,1,8]{2,1,0:T(1,128)S(1)}, u32[]{:S(2)}, u32[]{:S(2)}) async-start(f32[64,1,8]{2,1,0:T(1,128)} %bitcast.15), calls=%async_computation.6 | async-start | bytes 65536 | tf_op jit(solution)/shard_map/all_to_all | solution.py:85
  367.3 1.2 convolution_multiply_fusion
  368.5 11.1 %all-to-all-done.5 = f32[64,1,8]{2,1,0:T(1,128)S(1)} async-done(((f32[64,1,8]{2,1,0:T(1,128)}), f32[64,1,8]{2,1,0:T(1,128)S(1)}, u32[]{:S(2)}, u32[]{:S(2)}) %all-to-all-start.5) | async-done | bytes 2080 | tf_op jit(solution)/shard_map/all_to_all | solution.py:85
  379.6 23.8 %all-to-all-start.3 = ((f32[64,8,128]{2,1,0:T(8,128)}), f32[64,8,128]{2,1,0:T(8,128)S(1)}, u32[]{:S(2)}, u32[]{:S(2)}) async-start(f32[64,8,128]{2,1,0:T(8,128)} %convolution_multiply_fusion), calls=%async_computation.4 | async-start | bytes 524288 | tf_op jit(solution)/shard_map/all_to_all | solution.py:85
  403.4 0.1 reduce_sum.76
  403.5 20.0 %all-to-all-done.3 = f32[64,8,128]{2,1,0:T(8,128)S(1)} async-done(((f32[64,8,128]{2,1,0:T(8,128)}), f32[64,8,128]{2,1,0:T(8,128)S(1)}, u32[]{:S(2)}, u32[]{:S(2)}) %all-to-all-start.3) | async-done | bytes 262176 | tf_op jit(solution)/shard_map/all_to_all | solution.py:85
  423.4 0.6 broadcast_in_dim.80
  424.1 6.1 %all-to-all-start.6 = ((f32[64,1,8]{2,1,0:T(1,128)}), f32[64,1,8]{2,1,0:T(1,128)S(1)}, u32[]{:S(2)}, u32[]{:S(2)}) async-start(f32[64,1,8]{2,1,0:T(1,128)} %broadcast_in_dim.80), calls=%async_computation.7 | async-start | bytes 65536 | tf_op jit(solution)/shard_map/all_to_all | solution.py:13
  430.2 0.1 reduce_sum.74
  430.3 96.9 %all-to-all-done.6 = f32[64,1,8]{2,1,0:T(1,128)S(1)} async-done(((f32[64,1,8]{2,1,0:T(1,128)}), f32[64,1,8]{2,1,0:T(1,128)S(1)}, u32[]{:S(2)}, u32[]{:S(2)}) %all-to-all-start.6) | async-done | bytes 2080 | tf_op jit(solution)/shard_map/all_to_all | solution.py:13
  527.2 0.7 broadcast_in_dim.79
  527.9 4.2 all-to-all-start.4
  532.1 0.7 copy.19
  532.7 17.9 %all-to-all-done.4 = f32[64,8,128]{2,1,0:T(8,128)S(1)} async-done(((f32[64,8,128]{2,1,0:T(8,128)}), f32[64,8,128]{2,1,0:T(8,128)S(1)}, u32[]{:S(2)}, u32[]{:S(2)}) %all-to-all-start.4) | async-done | bytes 262176 | tf_op jit(solution)/shard_map/all_to_all | solution.py:13
  550.7 3.2 reduce_sum.77
  553.9 0.7 copy.41
  (61 shorter events, 0.8 us)
Async XLA Ops:
  7.2 146.9 %copy-start = (bf16[1024,128]{1,0:T(8,128)(2,1)S(1)}, bf16[1024,128]{1,0:T(8,128)(2,1)}, u32[]{:S(2)}) copy-start(bf16[1024,128]{1,0:T(8,128)(2,1)} %param.13) | copy-start | bytes 786436
  7.2 130.4 %copy-start.5 = (s32[64]{0:T(128)S(1)}, s32[64]{0:T(128)}, u32[]{:S(2)}) copy-start(s32[64]{0:T(128)} %param.15) | copy-start | bytes 772
  7.2 128.8 %all-gather.4.cloned.1.call-start = ((), (), s32[]{:S(2)}) async-start(), calls=%async_computation.8 | async-start | bytes 1331200 | tf_op jit(solution)/shard_map/all_gather | solution.py:133
  143.9 1.1 copy-start.2
  143.9 10.1 %copy-start.6 = (f32[64,8]{0,1:T(8,128)S(1)}, f32[64,8]{0,1:T(8,128)}, u32[]{:S(2)}) copy-start(f32[64,8]{0,1:T(8,128)} %param.14) | copy-start | bytes 6148
  144.0 10.1 %copy-start.3 = (bf16[64,8,128]{2,1,0:T(8,128)(2,1)S(1)}, bf16[64,8,128]{2,1,0:T(8,128)(2,1)}, u32[]{:S(2)}) copy-start(bf16[64,8,128]{2,1,0:T(8,128)(2,1)} %param.12) | copy-start | bytes 393220
  146.6 37.0 %all-to-all-start = ((f32[64,1,2048]{2,1,0:T(1,128)}), f32[64,1,2048]{2,1,0:T(1,128)S(1)}, u32[]{:S(2)}, u32[]{:S(2)}) async-start(f32[64,1,2048]{2,1,0:T(1,128)} %reshape.95), calls=%async_computation | async-start | bytes 1048576 | tf_op jit(solution)/shard_map/all_to_all | solution.py:13
  153.9 150.2 %reduce-scatter.2.cloned.1.call-start = ((), (), s32[]{:S(2)}) async-start(), calls=%async_computation.9 | async-start | bytes 589824 | tf_op jit(solution)/shard_map/reduce_scatter | solution.py:59
  183.6 0.8 copy-start.1
  196.9 154.5 %copy-start.4 = (bf16[64,8,128]{2,1,0:T(8,128)(2,1)S(1)}, bf16[64,8,128]{2,1,0:T(8,128)(2,1)}, u32[]{:S(2)}) copy-start(bf16[64,8,128]{2,1,0:T(8,128)(2,1)} %param.12) | copy-start | bytes 393220
  306.0 20.1 %all-to-all-start.1 = ((f32[64,2,8]{2,1,0:T(2,128)}), f32[64,2,8]{2,1,0:T(2,128)S(1)}, u32[]{:S(2)}, u32[]{:S(2)}) async-start(f32[64,2,8]{2,1,0:T(2,128)} %broadcast_in_dim.77), calls=%async_computation.2 | async-start | bytes 131072 | tf_op jit(solution)/shard_map/all_to_all | solution.py:13
  313.4 237.3 %all-gather.6.cloned.1.call-start = ((), (), s32[]{:S(2)}) async-start(), calls=%async_computation.10 | async-start | bytes 4718592 | tf_op jit(solution)/shard_map/all_gather | solution.py:193
  353.9 25.7 %all-to-all-start.5 = ((f32[64,1,8]{2,1,0:T(1,128)}), f32[64,1,8]{2,1,0:T(1,128)S(1)}, u32[]{:S(2)}, u32[]{:S(2)}) async-start(f32[64,1,8]{2,1,0:T(1,128)} %bitcast.15), calls=%async_computation.6 | async-start | bytes 65536 | tf_op jit(solution)/shard_map/all_to_all | solution.py:85
  379.6 43.9 %all-to-all-start.3 = ((f32[64,8,128]{2,1,0:T(8,128)}), f32[64,8,128]{2,1,0:T(8,128)S(1)}, u32[]{:S(2)}, u32[]{:S(2)}) async-start(f32[64,8,128]{2,1,0:T(8,128)} %convolution_multiply_fusion), calls=%async_computation.4 | async-start | bytes 524288 | tf_op jit(solution)/shard_map/all_to_all | solution.py:85
  424.1 103.1 %all-to-all-start.6 = ((f32[64,1,8]{2,1,0:T(1,128)}), f32[64,1,8]{2,1,0:T(1,128)S(1)}, u32[]{:S(2)}, u32[]{:S(2)}) async-start(f32[64,1,8]{2,1,0:T(1,128)} %broadcast_in_dim.80), calls=%async_computation.7 | async-start | bytes 65536 | tf_op jit(solution)/shard_map/all_to_all | solution.py:13
  527.9 22.8 %all-to-all-start.4 = ((f32[64,8,128]{2,1,0:T(8,128)}), f32[64,8,128]{2,1,0:T(8,128)S(1)}, u32[]{:S(2)}, u32[]{:S(2)}) async-start(f32[64,8,128]{2,1,0:T(8,128)} %broadcast_in_dim.79), calls=%async_computation.5 | async-start | bytes 524288 | tf_op jit(solution)/shard_map/all_to_all | solution.py:13
Sparse Core Ops, SparseCore 0:
  10.2 125.8 all-gather.3
  197.9 106.2 reduce-scatter.1
  353.0 186.7 all-gather.5
